TPU v7x, 32 devices: a whole 2x2x4 slice. The times are simulated.
32 devices in a mesh: ctx: 8 (over z, x), ch: 4 (over y, core).
Axes of the slice: x: 2, y: 2, z: 4, core: 2. Of those that a mesh axis runs over, the one named last changes fastest.
Arguments:
- tokens: bfloat16 [2048, 8192], P('ctx', 'ch'), may hold values from -6 to 6
- in_weight: bfloat16 [8192, 3, 8192], P('ctx', None, 'ch'), may hold values from -0.0625 to 0.0625
- short_filter: bfloat16 [3, 3, 8192], P(None, None, 'ch'), may hold values from -3 to 3
- decay_rate: float32 [8192, 16], P('ch'), may hold values from 2.4414063e-05 to 0.0333333333
- residue: float32 [8192, 16], P('ch'), may hold values from -0.12 to 0.12
- skip_gain: float32 [8192], P('ch'), may hold values from -4 to 4
Outputs:
- filtered: bfloat16 [2048, 8192], P('ctx', 'ch')
All inputs are finite; a program needn't handle non-finite values.
Results may differ from a plain program's by a relative error of at most 0.007.
Values may be sent and summed in bfloat16 or wider, within the bound.
A program may use at most 128 MiB of HBM per device.

v0:
```python
import jax
import jax.numpy as jnp
from jax import lax
from jax.sharding import PartitionSpec as P

exact_mode = lax.Precision.HIGHEST


def from_behind(block, axis, distance):
    devices = range(lax.axis_size(axis))
    route = [(i - distance, i) for i in devices if i - distance in devices]
    return lax.ppermute(block, axis, route)


def local(tokens, in_weight, short_filter, decay_rate, residue, skip_gain):
    tok_rows = tokens.shape[0]
    width_local = in_weight.shape[2]
    mode_count = decay_rate.shape[1]
    gathered = lax.all_gather(tokens, "ch", axis=1, tiled=True)
    feature_block = lax.all_to_all(gathered, "ctx", split_axis=1, concat_axis=0, tiled=True)
    flat_weight = in_weight.reshape(in_weight.shape[0], 3 * width_local)
    projected = lax.psum_scatter(
        jnp.dot(feature_block, flat_weight, preferred_element_type=jnp.float32),
        "ctx",
        scatter_dimension=0,
        tiled=True,
    )
    streams = projected.astype(jnp.bfloat16).reshape(tok_rows, 3, width_local)
    tap_count = short_filter.shape[0]
    last_rows = streams[tok_rows - (tap_count - 1) :]
    before = from_behind(last_rows, "ctx", 1)
    padded = jnp.concatenate([before, streams], axis=0).astype(jnp.float32)
    filter_taps = short_filter.astype(jnp.float32)
    featured = jnp.zeros((tok_rows, 3, width_local), jnp.float32)
    for shift_back in range(tap_count):
        begin = tap_count - 1 - shift_back
        featured = featured + filter_taps[shift_back][None] * padded[begin : begin + tok_rows]
    query_gate = featured[:, 0]
    gated_rows = (featured[:, 1] * featured[:, 2]).astype(jnp.bfloat16)
    gated_wide = gated_rows.astype(jnp.float32)
    position = jnp.arange(tok_rows, dtype=jnp.float32)
    powers = jnp.exp(-decay_rate[None, :, :] * (tok_rows - 1.0 - position)[:, None, None])
    zero_state = jnp.zeros(decay_rate.shape, jnp.float32)
    my_start = lax.axis_index("ctx") * tok_rows
    running = zero_state
    portion = lax.all_gather(gated_rows, "ctx", axis=0, tiled=True)
    count_blocks = portion.shape[0] // tok_rows
    shards = portion.reshape(count_blocks, tok_rows, portion.shape[1])

    def fold_block(carried, entry_pair):
        block_index, shard_rows = entry_pair
        block_start = block_index * tok_rows
        summary = jnp.einsum(
            "jc,jcr->cr", shard_rows.astype(jnp.float32), powers, precision=exact_mode
        )
        gap_rows = jnp.maximum(my_start - block_start - tok_rows, 0).astype(jnp.float32)
        factor = jnp.where(block_start < my_start, jnp.exp(-decay_rate * gap_rows), 0.0)
        return (carried + factor * summary, None)

    running, unused = lax.scan(
        fold_block, running, (jnp.arange(count_blocks, dtype=jnp.int32), shards)
    )
    growth = jnp.exp(decay_rate[None, :, :] * position[:, None, None])
    scaled = (gated_wide[:, :, None] * growth).reshape(tok_rows, width_local * mode_count)
    lower_mask = (jnp.arange(tok_rows)[:, None] >= jnp.arange(tok_rows)[None, :]).astype(
        jnp.float32
    )
    running_sum = jnp.dot(lower_mask, scaled, precision=exact_mode).reshape(
        tok_rows, width_local, mode_count
    )
    shrink = jnp.exp(-decay_rate[None, :, :] * position[:, None, None])
    entering = (running * jnp.exp(-decay_rate))[None]
    convolved = jnp.sum(residue[None] * shrink * (running_sum + entering), axis=2)
    long_mix = convolved + skip_gain[None, :] * gated_wide
    return (query_gate * long_mix).astype(jnp.bfloat16)


def solution(mesh):
    in_specs = (
        P("ctx", "ch"),
        P("ctx", None, "ch"),
        P(None, None, "ch"),
        P("ch", None),
        P("ch", None),
        P("ch"),
    )
    out_specs = P("ctx", "ch")
    return jax.shard_map(local, mesh=mesh, in_specs=in_specs, out_specs=out_specs, check_vma=False)
```

profile of v0, /device:TPU:0, one launch (start us, length us, event | category | flops | bytes accessed | tf_op | source)
XLA Modules:
  0.0 1251.9 jit_solution(11892983910678663819)
XLA Ops:
  6.5 2.3 copy.38
  8.8 0.0 all-gather.4.cloned.1.call-update
  8.8 37.3 %all-gather.4.cloned.1.call-done = bf16[256,8192]{0,1:T(8,128)(2,1)} async-done(((bf16[256,2048]{0,1:T(8,128)(2,1)}), bf16[256,8192]{0,1:T(8,128)(2,1)}) %all-gather.4.cloned.1.call-update) | async-done | bytes 4194320 | tf_op jit(solution)/shard_map/all_gather | solution.py:19
  46.2 5.5 all-to-all-start
  51.7 0.0 reduce-scatter.2.cloned.1.call-start
  51.7 16.6 %copy.40 = bf16[1024,3,2048]{0,2,1:T(8,128)(2,1)} copy(bf16[1024,3,2048]{2,0,1:T(8,128)(2,1)} %param.9) | data formatting | bytes 25165824 | tf_op args[1]
  68.3 77.0 %all-to-all-done = bf16[256,8,1024]{0,2,1:T(8,128)(2,1)} async-done(((bf16[256,8,1024]{0,2,1:T(8,128)(2,1)}), bf16[256,8,1024]{0,2,1:T(8,128)(2,1)}, u32[]{:S(2)}, u32[]{:S(2)}) %all-to-all-start) | async-done | bytes 4194336 | tf_op jit(solution)/shard_map/all_to_all | solution.py:20
  145.4 6.5 copy.39
  151.8 34.9 %fusion.14 = f32[2048,6144]{1,0:T(8,128)} fusion(bf16[2048,1024]{1,0:T(8,128)(2,1)} %bitcast.51, bf16[1024,6144]{0,1:T(8,128)(2,1)} %bitcast.48), kind=kOutput, calls=%fused_computation.27 | convolution fusion | flops 25769803776 | bytes 67108864 | tf_op jit(solution)/shard_map/dot_general | solution.py:23
  186.8 0.0 reduce-scatter.2.cloned.1.call-update
  186.8 0.0 all-gather.6.cloned.1.call-start
  186.8 0.7 copy-done.3
  187.6 787.2 %reduce-scatter.2.cloned.1.call-done = f32[256,6144]{1,0:T(8,128)} async-done(((f32[2048,6144]{1,0:T(8,128)}), f32[256,6144]{1,0:T(8,128)}) %reduce-scatter.2.cloned.1.call-update) | async-done | bytes 6291472 | tf_op jit(solution)/shard_map/reduce_scatter | solution.py:22
  974.7 3.2 convert_element_type.38
  978.0 3.6 collective-permute-start
  981.6 2.8 copy.42
  984.4 3.2 copy.43
  987.6 1.0 maximum_convert_fusion
  988.6 1.9 fusion.6
  990.5 2.7 copy-done
  993.2 1.3 bitcast_convert_fusion.1
  994.5 0.0 all-gather.6.cloned.1.call-update
  994.6 0.3 copy.45
  994.9 1.0 mul.161
  995.9 1.8 copy.44
  997.7 13.4 %bitcast_multiply_fusion = f32[256,32768]{0,1:T(8,128)} fusion(f32[32768]{0:T(1024)} %mul.161, f32[256,2048]{0,1:T(8,128)} %copy.44), kind=kLoop, calls=%fused_computation.4 | loop fusion | flops 16777216 | bytes 35782656 | tf_op jit(solution)/shard_map/mul | solution.py:64
  1011.1 106.7 %all-gather.6.cloned.1.call-done = bf16[2048,1,2048]{2,0,1:T(8,128)(2,1)} async-done(((bf16[256,1,2048]{2,0,1:T(8,128)(2,1)}), bf16[2048,1,2048]{2,0,1:T(8,128)(2,1)}) %all-gather.6.cloned.1.call-update) | async-done | bytes 8388624 | tf_op jit(solution)/shard_map/all_gather | solution.py:46
  1117.9 71.6 %while.15 = (s32[]{:T(128)}, f32[2048,16]{0,1:T(8,128)S(1)}, s32[8]{0:T(128)S(1)}, s32[]{:T(128)}, f32[2048,16]{0,1:T(8,128)S(1)}, /*index=5*/bf16[8,256,2048]{2...) while((s32[]{:T(128)}, f32[2048,16]{0,1:T(8,128)S(1)}, ...), condition=%wide.region_2.3_spmd.clone.clone.clone, body=%wide.region_1.2_spmd.clone.clone.clone.sunk | while | flops 25821184 | bytes 6030541 | solution.py:60
  1117.9 0.6 dynamic_slice.24
  1119.1 1.5 bitcast_convert_fusion.3
  1120.6 6.2 multiply_reduce_fusion.3
  1126.7 0.1 select_add_fusion.2
  1126.8 0.6 dynamic_slice.24
  1128.0 1.5 bitcast_convert_fusion.3
  1129.5 6.2 multiply_reduce_fusion.3
  1135.7 0.1 select_add_fusion.2
  1135.8 0.6 dynamic_slice.24
  1137.0 1.5 bitcast_convert_fusion.3
  1138.5 6.2 multiply_reduce_fusion.3
  1144.6 0.1 select_add_fusion.2
  1144.7 0.6 dynamic_slice.24
  1145.9 1.5 bitcast_convert_fusion.3
  1147.4 6.2 multiply_reduce_fusion.3
  1153.6 0.1 select_add_fusion.2
  1153.7 0.6 dynamic_slice.24
  1154.9 1.5 bitcast_convert_fusion.3
  1156.4 6.2 multiply_reduce_fusion.3
  1162.5 0.1 select_add_fusion.2
  1162.6 0.6 dynamic_slice.24
  1163.8 1.5 bitcast_convert_fusion.3
  1165.3 6.2 multiply_reduce_fusion.3
  1171.5 0.1 select_add_fusion.2
  1171.6 0.6 dynamic_slice.24
  1172.8 1.5 bitcast_convert_fusion.3
  1174.3 6.2 multiply_reduce_fusion.3
  1180.4 0.1 select_add_fusion.2
  1180.5 0.6 dynamic_slice.24
  1181.7 1.5 bitcast_convert_fusion.3
  1183.2 6.2 multiply_reduce_fusion.3
  1189.4 0.1 select_add_fusion.2
  1189.5 0.0 copy-start.1
  1189.5 0.0 copy-start.4
  1189.5 52.7 %multiply_reduce_fusion.1 = f32[256,2048]{1,0:T(8,128)S(1)} fusion(f32[2048,16,256]{2,1,0:T(8,128)} %bitcast.47, f32[2048,16]{0,1:T(8,128)S(1)} %exponential_multiply_fusion, f32[2048,16]{0,1:T(8,128)S(1)} %get-tuple-element.283, f32[2048,16]{0,1:T(8,128)S(1)} %copy-done.5), kind=kOutput, calls=%fused_computation.7 | convolution fusion | flops 25811288064 | bytes 36044800 | tf_op jit(solution)/shard_map/dot_general | solution.py:68
  1242.3 3.1 fusion.10
  (18 shorter events, 0.1 us)
Async XLA Ops:
  6.5 39.6 %all-gather.4.cloned.1.call-start = ((), (), s32[]{:S(2)}) async-start(), calls=%async_computation.2 | async-start | bytes 5242880 | tf_op jit(solution)/shard_map/all_gather | solution.py:19
  46.2 99.2 %all-to-all-start = ((bf16[256,8,1024]{0,2,1:T(8,128)(2,1)}), bf16[256,8,1024]{0,2,1:T(8,128)(2,1)}, u32[]{:S(2)}, u32[]{:S(2)}) async-start(bf16[256,8,1024]{0,2,1:T(8,128)(2,1)} %bitcast.50), calls=%async_computation | async-start | bytes 8388608 | tf_op jit(solution)/shard_map/all_to_all | solution.py:20
  51.7 923.1 %reduce-scatter.2.cloned.1.call-start = ((), (), s32[]{:S(2)}) async-start(), calls=%async_computation.3 | async-start | bytes 56623104 | tf_op jit(solution)/shard_map/reduce_scatter | solution.py:22
  186.8 0.8 copy-start.3
  186.8 931.1 %all-gather.6.cloned.1.call-start = ((), (), s32[]{:S(2)}) async-start(), calls=%async_computation.4 | async-start | bytes 9437184 | tf_op jit(solution)/shard_map/all_gather | solution.py:46
  978.0 9.6 collective-permute-start
  990.5 2.7 copy-start
  993.2 1.4 copy-start.2
  1117.9 71.6 %copy-start.5 = (f32[2048,16]{0,1:T(8,128)S(1)}, f32[2048,16]{0,1:T(8,128)}, u32[]{:S(2)}) copy-start(f32[2048,16]{0,1:T(8,128)} %param.12) | copy-start | bytes 393220
  1189.5 52.8 %copy-start.1 = (bf16[256,1,2048]{2,0,1:T(8,128)(2,1)S(1)}, bf16[256,1,2048]{2,0,1:T(8,128)(2,1)}, u32[]{:S(2)}) copy-start(bf16[256,1,2048]{2,0,1:T(8,128)(2,1)} %get-tuple-element.195) | copy-start | bytes 3145732
  1189.5 52.8 %copy-start.4 = (f32[2048]{0:T(1024)S(1)}, f32[2048]{0:T(1024)}, u32[]{:S(2)}) copy-start(f32[2048]{0:T(1024)} %param.13) | copy-start | bytes 24580
Sparse Core Ops, SparseCore 0:
  8.9 37.1 all-gather.3
  186.9 787.7 reduce-scatter.1
  994.7 123.1 all-gather.5
where the time goes:
time: 1250 us
  waiting for transfers between devices  1010 us (81%)
  matrix products  87.7 us (7%)
  other arithmetic  85.5 us (7%)
  local copies, waits for them, and re-layouts  42.7 us (3%)
  between operations  13.3 us (1%)
    reduce_scatter x1, waiting for transfers between devices, local(): lax.psum_scatter(jnp.dot(feature_block, flat_weight, preferred_element_ty...  787 us
    all_gather x1, waiting for transfers between devices, local(): portion = lax.all_gather(gated_rows, 'ctx', axis=0, tiled=True)  107 us
    all_to_all x1, waiting for transfers between devices, local(): lax.all_to_all(gathered, 'ctx', split_axis=1, concat_axis=0, tiled=True)  77 us
    dot_general x1, matrix products, local(): jnp.dot(lower_mask, scaled, precision=exact_mode)  52.7 us
    dot_general x8, other arithmetic, fold_block(): jnp.einsum('jc,jcr->cr', shard_rows.astype(jnp.float32), powers, precisio...  49.3 us
    all_gather x1, waiting for transfers between devices, local(): gathered = lax.all_gather(tokens, 'ch', axis=1, tiled=True)  37.3 us
    dot_general x1, matrix products, local(): jnp.dot(feature_block, flat_weight, preferred_element_type=jnp.float32)  34.9 us
  transfers between devices with their start and end apart: 5, of which 4 were waited for; matrix products, arithmetic and copies ran while one was open for 3% of the time, Pallas kernels for 0%

commit v1 on v0

v1 whole, which is shorter than its diff:
```python
import jax
import jax.numpy as jnp
from jax import lax
from jax.experimental import pallas as pl
from jax.experimental.pallas import tpu as pltpu
from jax.sharding import PartitionSpec as P

LINE = 4
VMEM_LIMIT = 40 * 1024 * 1024
STEPS = 8


def state_kernel(gated_ref, keep_ref, state_ref):
    modes = keep_ref.shape[0]

    def body(i, state):
        for u in range(STEPS):
            row = gated_ref[i * STEPS + u]
            state = tuple(keep_ref[m] * state[m] + row for m in range(modes))
        return state

    zero = jnp.zeros(keep_ref.shape[1:], jnp.float32)
    state = lax.fori_loop(0, gated_ref.shape[0] // STEPS, body, (zero,) * modes)
    for m in range(modes):
        state_ref[m] = state[m]


def mix_kernel(gated_ref, query_ref, keep_ref, residue_ref, skip_ref, enter_ref, out_ref):
    modes = keep_ref.shape[0]

    def body(i, state):
        for u in range(STEPS):
            t = i * STEPS + u
            row = gated_ref[t]
            state = tuple(keep_ref[m] * state[m] + row for m in range(modes))
            terms = [residue_ref[m] * state[m] for m in range(modes)]
            terms.append(skip_ref[...] * row)
            while len(terms) > 1:
                terms = [sum(terms[k : k + 2][1:], terms[k]) for k in range(0, len(terms), 2)]
            out_ref[t] = query_ref[t] * terms[0]
        return state

    start = tuple(enter_ref[m] for m in range(modes))
    lax.fori_loop(0, gated_ref.shape[0] // STEPS, body, start)


def call(kernel, out_shape, count):
    return pl.pallas_call(
        kernel,
        out_shape=jax.ShapeDtypeStruct(out_shape, jnp.float32),
        in_specs=[pl.BlockSpec(memory_space=pltpu.VMEM)] * count,
        out_specs=pl.BlockSpec(memory_space=pltpu.VMEM),
        compiler_params=pltpu.CompilerParams(vmem_limit_bytes=VMEM_LIMIT),
    )


def local(tokens, in_weight, short_filter, decay_rate, residue, skip_gain):
    n_ctx, n_ch = lax.axis_size("ctx"), lax.axis_size("ch")
    n_x = n_ctx // LINE
    n_q = n_ch // LINE
    me = lax.axis_index("ctx")
    z, x = me // n_x, me % n_x
    tok_rows = tokens.shape[0]
    feats, streams, width = in_weight.shape
    part = width // n_x
    rows = tok_rows * n_x
    modes = decay_rate.shape[1]

    def along_z(block, hop):
        route = [
            (i * n_x + k, (i + hop) * n_x + k)
            for i in range(LINE)
            if 0 <= i + hop < LINE
            for k in range(n_x)
        ]
        return lax.ppermute(block, "ctx", route)

    def along_x(block, hop):
        route = [
            (i * n_x + k, i * n_x + (k + hop) % n_x) for i in range(LINE) for k in range(n_x)
        ]
        return lax.ppermute(block, "ctx", route)

    def weight_part(g, index):
        return lax.dynamic_slice_in_dim(in_weight[:, g], index * part, part, axis=1)

    weights = [[None] * n_x for g in range(streams)]
    for g in range(streams):
        for hop in range(1, n_x):
            weights[g][hop] = along_x(weight_part(g, (x + hop) % n_x), hop)
        weights[g][0] = weight_part(g, x)

    route = [
        ((i * n_x + k) * n_ch + a * n_q + q, (a * n_x + k) * n_ch + i * n_q + q)
        for i in range(LINE)
        for k in range(n_x)
        for a in range(LINE)
        for q in range(n_q)
    ]
    moved = lax.ppermute(tokens, ("ctx", "ch"), route)
    groups = [[i * n_x + k for k in range(n_x)] for i in range(LINE)]
    moved = lax.all_gather(moved, "ctx", axis_index_groups=groups)
    moved = lax.all_gather(moved, "ch")
    moved = moved.reshape(LINE, n_q, n_x, tok_rows, tokens.shape[1])
    plane = moved.transpose(0, 2, 3, 1, 4).reshape(LINE, rows, n_x * feats)

    def columns(hop):
        return lax.dynamic_slice_in_dim(plane, ((x - hop) % n_x) * feats, feats, axis=2)

    columns_by_hop = [columns(hop) for hop in range(n_x)]

    def share(g, index):
        total = None
        for hop in range(n_x):
            block = lax.dynamic_index_in_dim(columns_by_hop[hop], index, 0, keepdims=False)
            term = jnp.dot(block, weights[g][hop], preferred_element_type=jnp.float32)
            total = term if total is None else total + term
        return total

    def choose(values):
        return jnp.array(values, jnp.int32)[z]

    first = choose([3, 3, 0, 0])
    second = choose([2, 3, 0, 1])
    third_up = choose([1, 2, 3, 3])
    third_down = choose([0, 0, 1, 2])

    def reduce_stream(g):
        low = jnp.bfloat16
        send = share(g, first).astype(low)
        up, down = along_z(send, 1), along_z(send, -1)
        mine = share(g, second)
        up = along_z((mine + up.astype(jnp.float32)).astype(low), 1)
        down = along_z((mine + down.astype(jnp.float32)).astype(low), -1)
        up = along_z((share(g, third_up) + up.astype(jnp.float32)).astype(low), 1)
        down = along_z((share(g, third_down) + down.astype(jnp.float32)).astype(low), -1)
        return share(g, z) + up.astype(jnp.float32) + down.astype(jnp.float32)

    taps = lax.dynamic_slice_in_dim(short_filter, x * part, part, axis=2).astype(jnp.float32)
    tap_count = taps.shape[0]
    featured = []
    for g in range(streams):
        projected = reduce_stream(g)
        before = along_z(projected[rows - (tap_count - 1) :], 1)
        padded = jnp.concatenate([before, projected], axis=0)
        total = jnp.zeros(projected.shape, jnp.float32)
        for back in range(tap_count):
            begin = tap_count - 1 - back
            total = total + taps[back, g][None] * padded[begin : begin + rows]
        featured.append(total)

    lanes = 128
    tile = (part // lanes, lanes)
    query = featured[0].reshape((rows,) + tile)
    gated = (featured[1] * featured[2]).reshape((rows,) + tile)

    def by_mode(array):
        mine = lax.dynamic_slice_in_dim(array, x * part, part, axis=0)
        return mine.T.reshape((modes,) + tile)

    rate, weight = by_mode(decay_rate), by_mode(residue)
    skip = lax.dynamic_slice_in_dim(skip_gain, x * part, part, axis=0).reshape(tile)
    keep = jnp.exp(-rate)
    state = call(state_kernel, (modes,) + tile, 2)(gated, keep)
    enter = jnp.zeros_like(state)
    for hop in range(1, LINE):
        enter = enter + along_z(state, hop) * jnp.exp(-rate * float((hop - 1) * rows))
    mixed = call(mix_kernel, (rows,) + tile, 6)(gated, query, keep, weight, skip, enter)
    mixed = mixed.reshape(n_x, tok_rows, part).astype(jnp.bfloat16)

    out = jnp.zeros((tok_rows, width), jnp.bfloat16)
    for hop in range(n_x):
        block = lax.dynamic_index_in_dim(mixed, (x + hop) % n_x, 0, keepdims=False)
        if hop:
            block = along_x(block, hop)
        out = lax.dynamic_update_slice_in_dim(out, block, ((x - hop) % n_x) * part, axis=1)
    return out


def solution(mesh):
    in_specs = (
        P("ctx", "ch"),
        P("ctx", None, "ch"),
        P(None, None, "ch"),
        P("ch", None),
        P("ch", None),
        P("ch"),
    )
    out_specs = P("ctx", "ch")
    return jax.shard_map(local, mesh=mesh, in_specs=in_specs, out_specs=out_specs, check_vma=False)
```

time: 1250 us -> 490 us (0.39)
  waiting for transfers between devices: 1010 us -> 259 us
  other arithmetic: 85.5 us -> 15.1 us
  starting transfers between devices: 9.16 us -> 70.6 us
  local copies, waits for them, and re-layouts: 42.7 us -> 17.5 us
    reduce_scatter x1 -> x0, waiting for transfers between devices: 787 us -> none  [local(): lax.psum_scatter(jnp.dot(feature_block, flat_weight, preferred_element_ty...]
    ppermute x1 -> x29, waiting for transfers between devices: 0.01 us -> 140 us  [the longest x24 83.8 us: along_z(): return lax.ppermute(block, 'ctx', route)]
    all_to_all x1 -> x0, waiting for transfers between devices: 77 us -> none  [local(): lax.all_to_all(gathered, 'ctx', split_axis=1, concat_axis=0, tiled=True)]
    ppermute x1 -> x29, starting transfers between devices: 3.57 us -> 70.6 us  [the longest x24 65.5 us: along_z(): return lax.ppermute(block, 'ctx', route)]
    dot_general x8 -> x0, other arithmetic: 49.3 us -> none  [fold_block(): jnp.einsum('jc,jcr->cr', shard_rows.astype(jnp.float32), powers, precisio...]
    all_gather x2, waiting for transfers between devices: 144 us -> 119 us  [the longest x1 83.4 us: local(): moved = lax.all_gather(moved, 'ctx', axis_index_groups=groups)]
    unnamed x15 -> x43, local copies, waits for them, and re-layouts: 22.6 us -> 3.53 us
    mul x2 -> x0, other arithmetic: 13.5 us -> none  [the longest x1 13.4 us: local(): gated_wide[:, :, None] * growth]
  transfers between devices with their start and end apart: 5 -> 31, of which waited for: 4 -> 17; matrix products, arithmetic and copies ran while one was open for 3% -> 25% of each run, Pallas kernels for 0% -> 0%
where the time goes in v1:
time: 490 us; the launch traced here: 483 us
  waiting for transfers between devices  259 us (53%)
  matrix products  91.5 us (19%)
  starting transfers between devices  70.6 us (14%)
  between operations  21.9 us (4%)
  local copies, waits for them, and re-layouts  17.5 us (4%)
  other arithmetic  15.1 us (3%)
  Pallas kernels  7.39 us (2%)
    dot_general x30, matrix products, share(): term = jnp.dot(block, weights[g][hop], preferred_element_type=jnp.float32)  91.5 us
    ppermute x24, waiting for transfers between devices, along_z(): return lax.ppermute(block, 'ctx', route)  83.8 us
    all_gather x1, waiting for transfers between devices, local(): moved = lax.all_gather(moved, 'ctx', axis_index_groups=groups)  83.4 us
    ppermute x24, starting transfers between devices, along_z(): return lax.ppermute(block, 'ctx', route)  65.5 us
    ppermute x4, waiting for transfers between devices, along_x(): return lax.ppermute(block, 'ctx', route)  56 us
    all_gather x1, waiting for transfers between devices, local(): moved = lax.all_gather(moved, 'ch')  36 us
  transfers between devices with their start and end apart: 31, of which 17 were waited for; matrix products, arithmetic and copies ran while one was open for 25% of the time, Pallas kernels for 0%

profile of v1, /device:TPU:0, one launch (start us, length us, event | category | flops | bytes accessed | tf_op | source)
XLA Modules:
  0.0 483.2 jit_solution(9460864931568598837)
XLA Ops:
  6.5 2.0 collective-permute-start
  9.6 83.4 %all-gather.5.cloned.1.call-done = bf16[512,2048]{1,0:T(8,128)(2,1)} async-done(((bf16[256,2048]{1,0:T(8,128)(2,1)}), bf16[512,2048]{1,0:T(8,128)(2,1)}) %all-gather.5.cloned.1.call-update) | async-done | bytes 2097168 | tf_op jit(solution)/shard_map/all_gather | solution.py:102
  93.0 5.8 %fusion.164 = (bf16[1024,1,2048]{2,0,1:T(8,128)(2,1)S(1)}, bf16[1024,1,2048]{2,0,1:T(8,128)(2,1)S(1)}, bf16[1024,1,2048]{2,0,1:T(8,128)(2,1)S(1)}) fusion(bf16[1024,3,2048]{2,0,1:T(8,128)(2,1)} %param.11), kind=kLoop, calls=%fused_computation.211 | loop fusion | bytes 25165824 | tf_op jit(solution)/shard_map/slice | solution.py:85
  98.9 1.7 dynamic-slice_bitcast_fusion.2
  100.9 2.2 dynamic-slice_bitcast_fusion.1
  103.1 1.8 collective-permute-start.9
  116.8 36.0 %all-gather.7.cloned.1.call-done = bf16[8,256,2048]{2,1,0:T(8,128)(2,1)} async-done(((bf16[2,256,2048]{2,1,0:T(8,128)(2,1)}), bf16[8,256,2048]{2,1,0:T(8,128)(2,1)}) %all-gather.7.cloned.1.call-update) | async-done | bytes 8388624 | tf_op jit(solution)/shard_map/all_gather | solution.py:103
  152.9 3.4 fusion.40
  156.3 3.4 add_convert_fusion.14
  159.7 3.4 collective-permute-start.2
  165.8 28.6 %collective-permute-done.9 = bf16[1024,1024]{1,0:T(8,128)(2,1)} collective-permute-done((bf16[1024,1024]{1,0:T(8,128)(2,1)}, bf16[1024,1024]{1,0:T(8,128)(2,1)}, u32[]{:S(2)}, u32[]{:S(2)}) %collective-permute-start.9) | collective-permute-done | bytes 2097184 | tf_op jit(solution)/shard_map/ppermute | solution.py:82
  194.4 3.9 add_convert_fusion.9
  198.3 3.4 collective-permute-start.10
  203.2 2.6 fusion.42
  205.8 2.6 fusion.32
  215.1 2.7 fusion.36
  217.8 2.6 fusion.20
  220.5 17.7 %collective-permute-done.17 = bf16[1024,1024]{1,0:T(8,128)(2,1)} collective-permute-done((bf16[1024,1024]{1,0:T(8,128)(2,1)S(1)}, bf16[1024,1024]{1,0:T(8,128)(2,1)}, u32[]{:S(2)}, u32[]{:S(2)}) %collective-permute-start.17) | collective-permute-done | bytes 2097184 | tf_op jit(solution)/shard_map/ppermute | solution.py:82
  238.2 4.2 add_convert_fusion.4
  242.4 3.7 collective-permute-start.18
  246.1 3.2 fusion.88
  249.3 3.2 fusion.97
  252.6 3.2 fusion.86
  255.8 3.2 fusion.65
  259.0 3.2 fusion.95
  262.3 3.2 fusion.84
  265.5 3.2 fusion.67
  268.7 2.6 fusion.24
  271.4 3.2 fusion.63
  274.6 4.0 fusion.22
  278.6 3.2 fusion.93
  283.5 5.7 %add_convert_fusion.13 = (bf16[512,1024]{1,0:T(8,128)(2,1)}, bf16[512,1024]{1,0:T(8,128)(2,1)}) fusion(bf16[512,1024]{1,0:T(8,128)(2,1)S(1)} %collective-permute-done.2, bf16[512,1024]{1,0:T(8,128)(2,1)} %collective-permute-done.5, f32[512,1024]{1,0:T(8,128)} %fusion.42, bf16[1024,1024]{1,0:T(8,128)(2,1)} %collective-permute-done.1, ...), kind=kOutput, calls=%fused_computation.75 | convolution fusion | flops 1077411840 | bytes 9437192 | tf_op jit(solution)/shard_map/dot_general | solution.py:116
  289.2 5.5 %collective-permute-start.3 = (bf16[512,1024]{1,0:T(8,128)(2,1)}, bf16[512,1024]{1,0:T(8,128)(2,1)}, u32[]{:S(2)}, u32[]{:S(2)}) collective-permute-start(bf16[512,1024]{1,0:T(8,128)(2,1)} %get-tuple-element.10), channel_id=1, source_target_pairs={{0,8},{4,12},{8,16},{12,20},{16,24},{20,28},{1,9},{5,13},{9,17},{1... | collective-permute-start | bytes 3145736 | tf_op jit(solution)/shard_map/ppermute | solution.py:76
  294.7 2.6 fusion.18
  298.7 5.7 %add_convert_fusion.8 = (bf16[512,1024]{1,0:T(8,128)(2,1)}, bf16[512,1024]{1,0:T(8,128)(2,1)}) fusion(bf16[512,1024]{1,0:T(8,128)(2,1)S(1)} %collective-permute-done.10, bf16[512,1024]{1,0:T(8,128)(2,1)} %collective-permute-done.13, f32[512,1024]{1,0:T(8,128)} %fusion.32, bf16[1024,1024]{1,0:T(8,128)(2,1)} %collective-permute-done.9, ...), kind=kOutput, calls=%fused_computation.68 | convolution fusion | flops 1077411840 | bytes 9437192 | tf_op jit(solution)/shard_map/dot_general | solution.py:116
  304.4 5.5 %collective-permute-start.11 = (bf16[512,1024]{1,0:T(8,128)(2,1)}, bf16[512,1024]{1,0:T(8,128)(2,1)}, u32[]{:S(2)}, u32[]{:S(2)}) collective-permute-start(bf16[512,1024]{1,0:T(8,128)(2,1)} %get-tuple-element.12), channel_id=1, source_target_pairs={{0,8},{4,12},{8,16},{12,20},{16,24},{20,28},{1,9},{5,13},{9,17},{1... | collective-permute-start | bytes 3145736 | tf_op jit(solution)/shard_map/ppermute | solution.py:76
  311.2 5.7 %add_convert_fusion.3 = (bf16[512,1024]{1,0:T(8,128)(2,1)}, bf16[512,1024]{1,0:T(8,128)(2,1)}) fusion(bf16[512,1024]{1,0:T(8,128)(2,1)S(1)} %collective-permute-done.18, bf16[512,1024]{1,0:T(8,128)(2,1)} %collective-permute-done.21, f32[512,1024]{1,0:T(8,128)} %fusion.22, bf16[1024,1024]{1,0:T(8,128)(2,1)} %collective-permute-done.17, ...), kind=kOutput, calls=%fused_computation.61 | convolution fusion | flops 1077411840 | bytes 9437192 | tf_op jit(solution)/shard_map/dot_general | solution.py:116
  316.9 5.5 %collective-permute-start.19 = (bf16[512,1024]{1,0:T(8,128)(2,1)}, bf16[512,1024]{1,0:T(8,128)(2,1)}, u32[]{:S(2)}, u32[]{:S(2)}) collective-permute-start(bf16[512,1024]{1,0:T(8,128)(2,1)} %get-tuple-element.8), channel_id=1, source_target_pairs={{0,8},{4,12},{8,16},{12,20},{16,24},{20,28},{1,9},{5,13},{9,17},{1... | collective-permute-start | bytes 3145736 | tf_op jit(solution)/shard_map/ppermute | solution.py:76
  323.7 2.8 add_convert_fusion.12
  326.5 6.1 %collective-permute-done.6 = bf16[512,1024]{1,0:T(8,128)(2,1)} collective-permute-done((bf16[512,1024]{1,0:T(8,128)(2,1)}, bf16[512,1024]{1,0:T(8,128)(2,1)}, u32[]{:S(2)}, u32[]{:S(2)}) %collective-permute-start.6) | collective-permute-done | bytes 1048608 | tf_op jit(solution)/shard_map/ppermute | solution.py:76
  332.6 3.4 collective-permute-start.4
  336.0 1.9 add_convert_fusion.10
  337.8 2.3 collective-permute-done.11
  341.4 1.9 add_convert_fusion.7
  343.3 11.7 %collective-permute-done.14 = bf16[512,1024]{1,0:T(8,128)(2,1)S(1)} collective-permute-done((bf16[512,1024]{1,0:T(8,128)(2,1)}, bf16[512,1024]{1,0:T(8,128)(2,1)S(1)}, u32[]{:S(2)}, u32[]{:S(2)}) %collective-permute-start.14) | collective-permute-done | bytes 1048608 | tf_op jit(solution)/shard_map/ppermute | solution.py:76
  355.0 3.4 collective-permute-start.12
  359.0 3.6 collective-permute-done.19
  363.9 1.9 add_convert_fusion.2
  365.8 11.8 %collective-permute-done.22 = bf16[512,1024]{1,0:T(8,128)(2,1)} collective-permute-done((bf16[512,1024]{1,0:T(8,128)(2,1)}, bf16[512,1024]{1,0:T(8,128)(2,1)}, u32[]{:S(2)}, u32[]{:S(2)}) %collective-permute-start.22) | collective-permute-done | bytes 1048608 | tf_op jit(solution)/shard_map/ppermute | solution.py:76
  377.5 3.4 collective-permute-start.20
  380.9 1.9 add_convert_fusion
  382.8 2.3 collective-permute-done.4
  386.4 2.6 fusion.26
  389.0 10.9 %collective-permute-done.7 = bf16[512,1024]{1,0:T(8,128)(2,1)S(1)} collective-permute-done((bf16[512,1024]{1,0:T(8,128)(2,1)S(1)}, bf16[512,1024]{1,0:T(8,128)(2,1)S(1)}, u32[]{:S(2)}, u32[]{:S(2)}) %collective-permute-start.7) | collective-permute-done | bytes 1048608 | tf_op jit(solution)/shard_map/ppermute | solution.py:76
  400.6 3.5 collective-permute-start.8
  404.1 3.4 collective-permute-done.12
  407.5 14.9 %collective-permute-done.15 = bf16[512,1024]{1,0:T(8,128)(2,1)S(1)} collective-permute-done((bf16[512,1024]{1,0:T(8,128)(2,1)S(1)}, bf16[512,1024]{1,0:T(8,128)(2,1)S(1)}, u32[]{:S(2)}, u32[]{:S(2)}) %collective-permute-start.15) | collective-permute-done | bytes 1048608 | tf_op jit(solution)/shard_map/ppermute | solution.py:76
  423.1 3.3 collective-permute-start.16
  427.5 15.0 %collective-permute-done.23 = bf16[512,1024]{1,0:T(8,128)(2,1)S(1)} collective-permute-done((bf16[512,1024]{1,0:T(8,128)(2,1)S(1)}, bf16[512,1024]{1,0:T(8,128)(2,1)S(1)}, u32[]{:S(2)}, u32[]{:S(2)}) %collective-permute-start.23) | collective-permute-done | bytes 1048608 | tf_op jit(solution)/shard_map/ppermute | solution.py:76
  443.2 3.3 collective-permute-start.24
  448.5 2.4 shard_map.100
  450.9 3.4 collective-permute-start.25
  458.8 5.0 %shard_map.101 = f32[512,8,128]{2,1,0:T(8,128)S(1)} custom-call(f32[512,8,128]{2,1,0:T(8,128)S(1)} %bitcast.189, f32[512,8,128]{2,1,0:T(8,128)S(1)} %bitcast.190, f32[16,8,128]{2,1,0:T(8,128)S(1)} %bitcast.192, f32[16,8,128]{2,1,0:T(8,128)S(1)} %bitcast.193, f32[8,128]{1,0:T(8,128)S(1)} %dynamic-slice_bitcast_fusion.5.skip_ref, ...), custom_call_target="tpu_custom_call" | custom-call | tf_op jit(solution)/shard_map/pallas_call | solution.py:168
  465.6 9.7 %collective-permute-done.28 = bf16[256,1024]{1,0:T(8,128)(2,1)S(1)} collective-permute-done((bf16[256,1024]{1,0:T(8,128)(2,1)S(1)}, bf16[256,1024]{1,0:T(8,128)(2,1)S(1)}, u32[]{:S(2)}, u32[]{:S(2)}) %collective-permute-start.28) | collective-permute-done | bytes 524320 | tf_op jit(solution)/shard_map/ppermute | solution.py:82
  (108 shorter events, 38.6 us)
Async XLA Ops:
  6.5 110.2 %copy-start = (f32[2048]{0:T(1024)S(1)}, f32[2048]{0:T(1024)}, u32[]{:S(2)}) copy-start(f32[2048]{0:T(1024)} %param.15) | copy-start | bytes 24580
  6.5 86.4 %all-gather.5.cloned.1.call-start = ((), (), s32[]{:S(2)}) async-start(), calls=%async_computation | async-start | bytes 3145728 | tf_op jit(solution)/shard_map/all_gather | solution.py:102
  6.5 2.0 collective-permute-start
  8.5 1.0 copy-start.8
  9.5 143.3 %all-gather.7.cloned.1.call-start = ((), (), s32[]{:S(2)}) async-start(), calls=%async_computation.1 | async-start | bytes 10485760 | tf_op jit(solution)/shard_map/all_gather | solution.py:103
  98.8 6.0 %copy-start.2 = (bf16[1024,1,2048]{2,0,1:T(8,128)(2,1)}, bf16[1024,1,2048]{2,0,1:T(8,128)(2,1)S(1)}, u32[]{:S(2)}) copy-start(bf16[1024,1,2048]{2,0,1:T(8,128)(2,1)S(1)} %get-tuple-element.5) | copy-start | bytes 12582916
  98.8 6.3 %copy-start.4 = (bf16[1024,1,2048]{2,0,1:T(8,128)(2,1)}, bf16[1024,1,2048]{2,0,1:T(8,128)(2,1)S(1)}, u32[]{:S(2)}) copy-start(bf16[1024,1,2048]{2,0,1:T(8,128)(2,1)S(1)} %get-tuple-element.7) | copy-start | bytes 12582916
  98.9 7.8 %copy-start.6 = (bf16[1024,1,2048]{2,0,1:T(8,128)(2,1)}, bf16[1024,1,2048]{2,0,1:T(8,128)(2,1)S(1)}, u32[]{:S(2)}) copy-start(bf16[1024,1,2048]{2,0,1:T(8,128)(2,1)S(1)} %get-tuple-element.6) | copy-start | bytes 12582916
  100.6 55.7 %collective-permute-start.1 = (bf16[1024,1024]{1,0:T(8,128)(2,1)}, bf16[1024,1024]{1,0:T(8,128)(2,1)}, u32[]{:S(2)}, u32[]{:S(2)}) collective-permute-start(bf16[1024,1024]{1,0:T(8,128)(2,1)} %dynamic-slice_bitcast_fusion.2), channel_id=1, source_target_pairs={{0,4},{4,0},{8,12},{12,8},{16,20},{20,16},{24,28},{28,24},{1,5},{5... | collective-permute-start | bytes 6291464 | tf_op jit(solution)/shard_map/ppermute | solution.py:82
  103.1 91.3 %collective-permute-start.9 = (bf16[1024,1024]{1,0:T(8,128)(2,1)}, bf16[1024,1024]{1,0:T(8,128)(2,1)}, u32[]{:S(2)}, u32[]{:S(2)}) collective-permute-start(bf16[1024,1024]{1,0:T(8,128)(2,1)} %dynamic-slice_bitcast_fusion.1), channel_id=1, source_target_pairs={{0,4},{4,0},{8,12},{12,8},{16,20},{20,16},{24,28},{28,24},{1,5},{5... | collective-permute-start | bytes 6291464 | tf_op jit(solution)/shard_map/ppermute | solution.py:82
  104.9 1.8 copy-start.17
  104.9 3.7 copy-start.16
  104.9 5.4 %copy-start.15 = (s32[4]{0:T(128)S(1)}, s32[4]{0:T(128)}, u32[]{:S(2)}) copy-start(s32[4]{0:T(128)} %constant.306.clone) | copy-start | bytes 52
  104.9 7.1 %copy-start.14 = (s32[4]{0:T(128)S(1)}, s32[4]{0:T(128)}, u32[]{:S(2)}) copy-start(s32[4]{0:T(128)} %constant.307.clone) | copy-start | bytes 52
  104.9 11.7 %copy-start.10 = (f32[2048,16]{0,1:T(8,128)S(1)}, f32[2048,16]{0,1:T(8,128)}, u32[]{:S(2)}) copy-start(f32[2048,16]{0,1:T(8,128)} %param.13) | copy-start | bytes 393220
  104.9 11.7 %copy-start.11 = (f32[2048,16]{0,1:T(8,128)S(1)}, f32[2048,16]{0,1:T(8,128)}, u32[]{:S(2)}) copy-start(f32[2048,16]{0,1:T(8,128)} %param.14) | copy-start | bytes 393220
  104.9 11.9 %copy-start.12 = (bf16[3,3,2048]{2,1,0:T(4,128)(2,1)S(1)}, bf16[3,3,2048]{2,1,0:T(4,128)(2,1)}, u32[]{:S(2)}) copy-start(bf16[3,3,2048]{2,1,0:T(4,128)(2,1)} %param.12) | copy-start | bytes 110596
  106.7 131.5 %collective-permute-start.17 = (bf16[1024,1024]{1,0:T(8,128)(2,1)S(1)}, bf16[1024,1024]{1,0:T(8,128)(2,1)}, u32[]{:S(2)}, u32[]{:S(2)}) collective-permute-start(bf16[1024,1024]{1,0:T(8,128)(2,1)S(1)} %dynamic-slice_bitcast_fusion), channel_id=1, source_target_pairs={{0,4},{4,0},{8,12},{12,8},{16,20},{20,16},{24,28},{28,24},{1,5},{5... | collective-permute-start | bytes 6291464 | tf_op jit(solution)/shard_map/ppermute | solution.py:82
  152.9 11.6 %copy-start.13 = (bf16[8,256,2048]{2,1,0:T(8,128)(2,1)S(1)}, bf16[8,256,2048]{2,1,0:T(8,128)(2,1)}, u32[]{:S(2)}) copy-start(bf16[8,256,2048]{2,1,0:T(8,128)(2,1)} %all-gather.7.cloned.1.call-done) | copy-start | bytes 25165828
  156.3 8.2 %copy-start.5 = (bf16[1024,1,2048]{2,0,1:T(8,128)(2,1)S(1)}, bf16[1024,1,2048]{2,0,1:T(8,128)(2,1)}, u32[]{:S(2)}) copy-start(bf16[1024,1,2048]{2,0,1:T(8,128)(2,1)} %copy-done.4) | copy-start | bytes 12582916
  159.7 122.1 %collective-permute-start.2 = (bf16[512,1024]{1,0:T(8,128)(2,1)S(1)}, bf16[512,1024]{1,0:T(8,128)(2,1)S(1)}, u32[]{:S(2)}, u32[]{:S(2)}) collective-permute-start(bf16[512,1024]{1,0:T(8,128)(2,1)S(1)} %add_convert_fusion.14), channel_id=1, source_target_pairs={{0,8},{4,12},{8,16},{12,20},{16,24},{20,28},{1,9},{5,13},{9,17},{1... | collective-permute-start | bytes 3145736 | tf_op jit(solution)/shard_map/ppermute | solution.py:76
  163.1 120.4 %collective-permute-start.5 = (bf16[512,1024]{1,0:T(8,128)(2,1)S(1)}, bf16[512,1024]{1,0:T(8,128)(2,1)}, u32[]{:S(2)}, u32[]{:S(2)}) collective-permute-start(bf16[512,1024]{1,0:T(8,128)(2,1)S(1)} %add_convert_fusion.14), channel_id=1, source_target_pairs={{8,0},{12,4},{16,8},{20,12},{24,16},{28,20},{9,1},{13,5},{17,9},{2... | collective-permute-start | bytes 3145736 | tf_op jit(solution)/shard_map/ppermute | solution.py:76
  165.8 37.4 %copy-start.7 = (bf16[1024,1,2048]{2,0,1:T(8,128)(2,1)S(1)}, bf16[1024,1,2048]{2,0,1:T(8,128)(2,1)}, u32[]{:S(2)}) copy-start(bf16[1024,1,2048]{2,0,1:T(8,128)(2,1)} %copy-done.6) | copy-start | bytes 12582916
  198.3 99.1 %collective-permute-start.10 = (bf16[512,1024]{1,0:T(8,128)(2,1)}, bf16[512,1024]{1,0:T(8,128)(2,1)S(1)}, u32[]{:S(2)}, u32[]{:S(2)}) collective-permute-start(bf16[512,1024]{1,0:T(8,128)(2,1)} %add_convert_fusion.9), channel_id=1, source_target_pairs={{0,8},{4,12},{8,16},{12,20},{16,24},{20,28},{1,9},{5,13},{9,17},{1... | collective-permute-start | bytes 3145736 | tf_op jit(solution)/shard_map/ppermute | solution.py:76
  201.7 96.9 %collective-permute-start.13 = (bf16[512,1024]{1,0:T(8,128)(2,1)}, bf16[512,1024]{1,0:T(8,128)(2,1)}, u32[]{:S(2)}, u32[]{:S(2)}) collective-permute-start(bf16[512,1024]{1,0:T(8,128)(2,1)} %add_convert_fusion.9), channel_id=1, source_target_pairs={{8,0},{12,4},{16,8},{20,12},{24,16},{28,20},{9,1},{13,5},{17,9},{2... | collective-permute-start | bytes 3145736 | tf_op jit(solution)/shard_map/ppermute | solution.py:76
  215.1 2.7 copy-start.3
  242.4 67.5 %collective-permute-start.18 = (bf16[512,1024]{1,0:T(8,128)(2,1)}, bf16[512,1024]{1,0:T(8,128)(2,1)S(1)}, u32[]{:S(2)}, u32[]{:S(2)}) collective-permute-start(bf16[512,1024]{1,0:T(8,128)(2,1)} %add_convert_fusion.4), channel_id=1, source_target_pairs={{0,8},{4,12},{8,16},{12,20},{16,24},{20,28},{1,9},{5,13},{9,17},{1... | collective-permute-start | bytes 3145736 | tf_op jit(solution)/shard_map/ppermute | solution.py:76
  281.8 29.4 %collective-permute-start.21 = (bf16[512,1024]{1,0:T(8,128)(2,1)}, bf16[512,1024]{1,0:T(8,128)(2,1)}, u32[]{:S(2)}, u32[]{:S(2)}) collective-permute-start(bf16[512,1024]{1,0:T(8,128)(2,1)} %add_convert_fusion.4), channel_id=1, source_target_pairs={{8,0},{12,4},{16,8},{20,12},{24,16},{28,20},{9,1},{13,5},{17,9},{2... | collective-permute-start | bytes 3145736 | tf_op jit(solution)/shard_map/ppermute | solution.py:76
  289.2 33.2 %collective-permute-start.3 = (bf16[512,1024]{1,0:T(8,128)(2,1)}, bf16[512,1024]{1,0:T(8,128)(2,1)}, u32[]{:S(2)}, u32[]{:S(2)}) collective-permute-start(bf16[512,1024]{1,0:T(8,128)(2,1)} %get-tuple-element.10), channel_id=1, source_target_pairs={{0,8},{4,12},{8,16},{12,20},{16,24},{20,28},{1,9},{5,13},{9,17},{1... | collective-permute-start | bytes 3145736 | tf_op jit(solution)/shard_map/ppermute | solution.py:76
  297.4 35.2 %collective-permute-start.6 = (bf16[512,1024]{1,0:T(8,128)(2,1)}, bf16[512,1024]{1,0:T(8,128)(2,1)}, u32[]{:S(2)}, u32[]{:S(2)}) collective-permute-start(bf16[512,1024]{1,0:T(8,128)(2,1)} %get-tuple-element.11), channel_id=1, source_target_pairs={{8,0},{12,4},{16,8},{20,12},{24,16},{28,20},{9,1},{13,5},{17,9},{2... | collective-permute-start | bytes 3145736 | tf_op jit(solution)/shard_map/ppermute | solution.py:76
  304.4 35.8 %collective-permute-start.11 = (bf16[512,1024]{1,0:T(8,128)(2,1)}, bf16[512,1024]{1,0:T(8,128)(2,1)}, u32[]{:S(2)}, u32[]{:S(2)}) collective-permute-start(bf16[512,1024]{1,0:T(8,128)(2,1)} %get-tuple-element.12), channel_id=1, source_target_pairs={{0,8},{4,12},{8,16},{12,20},{16,24},{20,28},{1,9},{5,13},{9,17},{1... | collective-permute-start | bytes 3145736 | tf_op jit(solution)/shard_map/ppermute | solution.py:76
  309.9 45.0 %collective-permute-start.14 = (bf16[512,1024]{1,0:T(8,128)(2,1)}, bf16[512,1024]{1,0:T(8,128)(2,1)S(1)}, u32[]{:S(2)}, u32[]{:S(2)}) collective-permute-start(bf16[512,1024]{1,0:T(8,128)(2,1)} %get-tuple-element.13), channel_id=1, source_target_pairs={{8,0},{12,4},{16,8},{20,12},{24,16},{28,20},{9,1},{13,5},{17,9},{2... | collective-permute-start | bytes 3145736 | tf_op jit(solution)/shard_map/ppermute | solution.py:76
  316.9 45.7 %collective-permute-start.19 = (bf16[512,1024]{1,0:T(8,128)(2,1)}, bf16[512,1024]{1,0:T(8,128)(2,1)}, u32[]{:S(2)}, u32[]{:S(2)}) collective-permute-start(bf16[512,1024]{1,0:T(8,128)(2,1)} %get-tuple-element.8), channel_id=1, source_target_pairs={{0,8},{4,12},{8,16},{12,20},{16,24},{20,28},{1,9},{5,13},{9,17},{1... | collective-permute-start | bytes 3145736 | tf_op jit(solution)/shard_map/ppermute | solution.py:76
  322.4 55.1 %collective-permute-start.22 = (bf16[512,1024]{1,0:T(8,128)(2,1)}, bf16[512,1024]{1,0:T(8,128)(2,1)}, u32[]{:S(2)}, u32[]{:S(2)}) collective-permute-start(bf16[512,1024]{1,0:T(8,128)(2,1)} %get-tuple-element.9), channel_id=1, source_target_pairs={{8,0},{12,4},{16,8},{20,12},{24,16},{28,20},{9,1},{13,5},{17,9},{2... | collective-permute-start | bytes 3145736 | tf_op jit(solution)/shard_map/ppermute | solution.py:76
  332.6 52.5 %collective-permute-start.4 = (bf16[512,1024]{1,0:T(8,128)(2,1)}, bf16[512,1024]{1,0:T(8,128)(2,1)S(1)}, u32[]{:S(2)}, u32[]{:S(2)}) collective-permute-start(bf16[512,1024]{1,0:T(8,128)(2,1)} %add_convert_fusion.12), channel_id=1, source_target_pairs={{0,8},{4,12},{8,16},{12,20},{16,24},{20,28},{1,9},{5,13},{9,17},{1... | collective-permute-start | bytes 3145736 | tf_op jit(solution)/shard_map/ppermute | solution.py:76
  340.2 59.8 %collective-permute-start.7 = (bf16[512,1024]{1,0:T(8,128)(2,1)S(1)}, bf16[512,1024]{1,0:T(8,128)(2,1)S(1)}, u32[]{:S(2)}, u32[]{:S(2)}) collective-permute-start(bf16[512,1024]{1,0:T(8,128)(2,1)S(1)} %add_convert_fusion.10), channel_id=1, source_target_pairs={{8,0},{12,4},{16,8},{20,12},{24,16},{28,20},{9,1},{13,5},{17,9},{2... | collective-permute-start | bytes 3145736 | tf_op jit(solution)/shard_map/ppermute | solution.py:76
  355.0 52.5 %collective-permute-start.12 = (bf16[512,1024]{1,0:T(8,128)(2,1)S(1)}, bf16[512,1024]{1,0:T(8,128)(2,1)S(1)}, u32[]{:S(2)}, u32[]{:S(2)}) collective-permute-start(bf16[512,1024]{1,0:T(8,128)(2,1)S(1)} %add_convert_fusion.7), channel_id=1, source_target_pairs={{0,8},{4,12},{8,16},{12,20},{16,24},{20,28},{1,9},{5,13},{9,17},{1... | collective-permute-start | bytes 3145736 | tf_op jit(solution)/shard_map/ppermute | solution.py:76
  362.6 59.8 %collective-permute-start.15 = (bf16[512,1024]{1,0:T(8,128)(2,1)S(1)}, bf16[512,1024]{1,0:T(8,128)(2,1)S(1)}, u32[]{:S(2)}, u32[]{:S(2)}) collective-permute-start(bf16[512,1024]{1,0:T(8,128)(2,1)S(1)} %add_convert_fusion.5), channel_id=1, source_target_pairs={{8,0},{12,4},{16,8},{20,12},{24,16},{28,20},{9,1},{13,5},{17,9},{2... | collective-permute-start | bytes 3145736 | tf_op jit(solution)/shard_map/ppermute | solution.py:76
  377.5 49.9 %collective-permute-start.20 = (bf16[512,1024]{1,0:T(8,128)(2,1)S(1)}, bf16[512,1024]{1,0:T(8,128)(2,1)S(1)}, u32[]{:S(2)}, u32[]{:S(2)}) collective-permute-start(bf16[512,1024]{1,0:T(8,128)(2,1)S(1)} %add_convert_fusion.2), channel_id=1, source_target_pairs={{0,8},{4,12},{8,16},{12,20},{16,24},{20,28},{1,9},{5,13},{9,17},{1... | collective-permute-start | bytes 3145736 | tf_op jit(solution)/shard_map/ppermute | solution.py:76
  385.1 57.4 %collective-permute-start.23 = (bf16[512,1024]{1,0:T(8,128)(2,1)S(1)}, bf16[512,1024]{1,0:T(8,128)(2,1)S(1)}, u32[]{:S(2)}, u32[]{:S(2)}) collective-permute-start(bf16[512,1024]{1,0:T(8,128)(2,1)S(1)} %add_convert_fusion), channel_id=1, source_target_pairs={{8,0},{12,4},{16,8},{20,12},{24,16},{28,20},{9,1},{13,5},{17,9},{2... | collective-permute-start | bytes 3145736 | tf_op jit(solution)/shard_map/ppermute | solution.py:76
  400.6 46.0 %collective-permute-start.8 = (f32[2,1024]{1,0:T(2,128)S(1)}, f32[2,1024]{1,0:T(2,128)S(1)}, u32[]{:S(2)}, u32[]{:S(2)}) collective-permute-start(f32[2,1024]{1,0:T(2,128)S(1)} %slice.89), channel_id=1, source_target_pairs={{0,8},{4,12},{8,16},{12,20},{16,24},{20,28},{1,9},{5,13},{9,17},{1... | collective-permute-start | bytes 24584 | tf_op jit(solution)/shard_map/ppermute | solution.py:76
  423.1 23.5 %collective-permute-start.16 = (f32[2,1024]{1,0:T(2,128)S(1)}, f32[2,1024]{1,0:T(2,128)S(1)}, u32[]{:S(2)}, u32[]{:S(2)}) collective-permute-start(f32[2,1024]{1,0:T(2,128)S(1)} %slice.95), channel_id=1, source_target_pairs={{0,8},{4,12},{8,16},{12,20},{16,24},{20,28},{1,9},{5,13},{9,17},{1... | collective-permute-start | bytes 24584 | tf_op jit(solution)/shard_map/ppermute | solution.py:76
  443.2 13.7 %collective-permute-start.24 = (f32[2,1024]{1,0:T(2,128)S(1)}, f32[2,1024]{1,0:T(2,128)S(1)}, u32[]{:S(2)}, u32[]{:S(2)}) collective-permute-start(f32[2,1024]{1,0:T(2,128)S(1)} %slice.101), channel_id=1, source_target_pairs={{0,8},{4,12},{8,16},{12,20},{16,24},{20,28},{1,9},{5,13},{9,17},{1... | collective-permute-start | bytes 24584 | tf_op jit(solution)/shard_map/ppermute | solution.py:76
  450.9 7.2 %collective-permute-start.25 = (f32[16,8,128]{2,1,0:T(8,128)S(1)}, f32[16,8,128]{2,1,0:T(8,128)S(1)}, u32[]{:S(2)}, u32[]{:S(2)}) collective-permute-start(f32[16,8,128]{2,1,0:T(8,128)S(1)} %shard_map.100), channel_id=1, source_target_pairs={{0,8},{4,12},{8,16},{12,20},{16,24},{20,28},{1,9},{5,13},{9,17},{1... | collective-permute-start | bytes 196616 | tf_op jit(solution)/shard_map/ppermute | solution.py:76
  454.2 3.8 collective-permute-start.26
  455.6 3.2 collective-permute-start.27
  464.0 12.2 %copy-start.1 = (f32[2048]{0:T(1024)S(1)}, f32[2048]{0:T(1024)}, u32[]{:S(2)}) copy-start(f32[2048]{0:T(1024)} %param.15) | copy-start | bytes 24580
  464.5 10.8 %collective-permute-start.28 = (bf16[256,1024]{1,0:T(8,128)(2,1)S(1)}, bf16[256,1024]{1,0:T(8,128)(2,1)S(1)}, u32[]{:S(2)}, u32[]{:S(2)}) collective-permute-start(bf16[256,1024]{1,0:T(8,128)(2,1)S(1)} %dynamic-slice_bitcast_fusion.3), channel_id=1, source_target_pairs={{0,4},{4,0},{8,12},{12,8},{16,20},{20,16},{24,28},{28,24},{1,5},{5... | collective-permute-start | bytes 1572872 | tf_op jit(solution)/shard_map/ppermute | solution.py:82
  465.6 9.7 %copy-start.9 = (bf16[256,2048]{1,0:T(8,128)(2,1)}, bf16[256,2048]{1,0:T(8,128)(2,1)S(1)}, u32[]{:S(2)}) copy-start(bf16[256,2048]{1,0:T(8,128)(2,1)S(1)} %bitcast_dynamic-update-slice_fusion) | copy-start | bytes 3145732
Sparse Core Ops, SparseCore 0:
  9.7 83.2 all-gather.4
  94.5 58.2 all-gather.6
